TPU v7x, 768 devices: a whole 4x8x12 slice. The times are simulated.
768 devices in a mesh: row: 384 (over z, y, x), col: 2 (over core).
Axes of the slice: x: 4, y: 8, z: 12, core: 2. Of those that a mesh axis runs over, the one named last changes fastest.
Arguments:
- three_center: bfloat16 [12288, 128, 512], P('row', None, 'col'), may hold values from -6 to 6
- screen_mask: int32 [12288, 2], P('row'), may hold values 0 or 1
- green_occ: bfloat16 [128, 128], replicated, may hold values from -0.5 to 0.5
- green_virt: bfloat16 [128, 128], replicated, may hold values from -0.5 to 0.5
Outputs:
- polariz: float32 [512, 512], P('col')
All inputs are finite; a program needn't handle non-finite values. No bound on the sum of `screen_mask` on one device may be relied on, other than what follows from the above.
Results may differ from a plain program's by a relative error of at most 0.0041.
Values may be sent and summed in bfloat16 or wider, within the bound.
No kernel may reach another device: no remote copies, remote signals or barrier semaphores. Data moves between devices by JAX's collectives and lax.ppermute only.
A program may use at most 32 MiB of HBM per device.

v0:
```python
import jax
import jax.numpy as jnp
from jax import lax
from jax.sharding import PartitionSpec as P


def contract(green, screened):
    return jnp.einsum("sn,mnp->msp", green, screened, preferred_element_type=jnp.float32).astype(
        jnp.bfloat16
    )


def on_device(three_center, screen_mask, green_occ, green_virt):
    mu_dev, width, p_dev = three_center.shape
    blocks = screen_mask.shape[1]
    keep = jnp.repeat(screen_mask, width // blocks, axis=1).astype(jnp.bfloat16)
    screened = three_center * keep[:, :, None]
    moved = lax.all_to_all(screened, "col", split_axis=0, concat_axis=2, tiled=True)
    occ_side = contract(green_occ, moved)
    virt_side = contract(green_virt, moved)
    partial_sum = lax.psum_scatter(
        jnp.einsum("msp,msq->pq", occ_side, virt_side, preferred_element_type=jnp.float32),
        "col",
        scatter_dimension=0,
        tiled=True,
    )
    summed = lax.psum(partial_sum, "row")
    nmu_total = mu_dev * lax.axis_size("row")
    return -summed / jnp.sqrt(jnp.float32(nmu_total * width))


def solution(mesh):
    return jax.shard_map(
        on_device,
        mesh=mesh,
        in_specs=(P("row", None, "col"), P("row", None), P(), P()),
        out_specs=P("col", None),
        check_vma=False,
    )
```

profile of v0, /device:TPU:2, one launch (start us, length us, event | category | flops | bytes accessed | tf_op | source)
XLA Modules:
  0.0 447.5 jit_solution(10571411647001443675)
XLA Ops:
  6.5 0.0 copy-start
  6.5 0.0 reduce-scatter.2.cloned.1.call-start
  6.5 0.7 convert_element_type.23
  7.2 0.1 copy.7
  7.3 0.1 broadcast_in_dim.4
  7.4 0.1 convert_element_type.24
  7.5 1.9 broadcast_multiply_fusion
  9.5 5.4 %all_to_all.18 = bf16[32,128,256]{2,1,0:T(8,128)(2,1)S(1)} all-to-all(bf16[32,128,256]{2,1,0:T(8,128)(2,1)S(1)} %broadcast_multiply_fusion), channel_id=1, replica_groups=mesh['row'=384,'col'=2] {'col'}, dimensions={0} | all-to-all | bytes 4194304 | tf_op jit(solution)/shard_map/all_to_all | solution.py:18
  14.9 0.0 copy-start.1
  14.9 2.4 copy.8
  17.3 0.0 copy-done
  17.3 0.0 copy-done.1
  17.3 5.6 %fusion.9 = f32[512,512]{1,0:T(8,128)} fusion(bf16[16,128,512]{1,2,0:T(8,128)(2,1)} %bitcast.27, bf16[128,128]{1,0:T(8,128)(2,1)S(1)} %copy-done, bf16[128,128]{1,0:T(8,128)(2,1)S(1)} %copy-done.1), kind=kOutput, calls=%fused_computation.7 | convolution fusion | flops 1612709888 | bytes 3211264 | tf_op jit(solution)/shard_map/msp,msq->pq/dot_general | solution.py:22
  22.8 0.0 reduce-scatter.2.cloned.1.call-update
  22.9 0.0 all-reduce.2.cloned.1.call-start
  22.9 26.2 %reduce-scatter.2.cloned.1.call-done = f32[256,512]{1,0:T(8,128)} async-done(((f32[512,512]{1,0:T(8,128)}), f32[256,512]{1,0:T(8,128)}) %reduce-scatter.2.cloned.1.call-update) | async-done | bytes 524304 | tf_op jit(solution)/shard_map/reduce_scatter | solution.py:21
  49.1 0.0 all-reduce.2.cloned.1.call-update
  49.1 389.6 %all-reduce.2.cloned.1.call-done = f32[256,512]{1,0:T(8,128)} async-done(((f32[256,512]{1,0:T(8,128)}), f32[256,512]{1,0:T(8,128)}) %all-reduce.2.cloned.1.call-update) | async-done | bytes 524304 | tf_op jit(solution)/shard_map/psum | solution.py:27
  438.7 1.9 negate_multiply_fusion
Async XLA Ops:
  6.5 10.7 %copy-start = (bf16[128,128]{1,0:T(8,128)(2,1)S(1)}, bf16[128,128]{1,0:T(8,128)(2,1)}, u32[]{:S(2)}) copy-start(bf16[128,128]{1,0:T(8,128)(2,1)} %param.7) | copy-start | bytes 98308
  6.5 42.6 %reduce-scatter.2.cloned.1.call-start = ((), (), s32[]{:S(2)}) async-start(), calls=%async_computation.2 | async-start | bytes 1572864 | tf_op jit(solution)/shard_map/reduce_scatter | solution.py:21
  14.9 2.4 copy-start.1
  22.9 415.9 %all-reduce.2.cloned.1.call-start = ((), (), s32[]{:S(2)}) async-start(), calls=%async_computation.3 | async-start | bytes 1048576 | tf_op jit(solution)/shard_map/psum | solution.py:27
Sparse Core Ops, SparseCore 0:
  23.0 26.0 reduce-scatter.1
  55.3 383.4 all-reduce.1
where the time goes:
time: 448 us; the launch traced here: 447 us
  waiting for transfers between devices  416 us (93%)
  between operations  13.4 us (3%)
  matrix products  5.56 us (1%)
  blocking collectives  5.42 us (1%)
  other arithmetic  4.51 us (1%)
    psum x1, waiting for transfers between devices, on_device(): summed = lax.psum(partial_sum, 'row')  390 us
    reduce_scatter x1, waiting for transfers between devices, on_device(): lax.psum_scatter(jnp.einsum('msp,msq->pq', occ_side, virt_side, preferred...  26.2 us
  transfers between devices with their start and end apart: 2, of which 2 were waited for; matrix products, arithmetic and copies ran while one was open for 0% of the time, Pallas kernels for 0%

commit v1 on v0

v1 whole, which is shorter than its diff:
```python
import jax
import jax.numpy as jnp
from jax import lax
from jax.sharding import Mesh, PartitionSpec as P

Z, YX = 12, 32


def contract(green, screened):
    return jnp.einsum("sn,mnp->msp", green, screened, preferred_element_type=jnp.float32).astype(
        jnp.bfloat16
    )


def pair(occ_side, virt_side):
    return jnp.einsum("msp,msq->pq", occ_side, virt_side, preferred_element_type=jnp.float32)


def sum_over_row(partial):
    rows, columns = partial.shape
    pieces = partial.astype(jnp.bfloat16).reshape(YX, rows // YX, columns)
    pieces = lax.all_to_all(pieces, "yx", 0, 0, tiled=True)
    piece = jnp.sum(pieces.astype(jnp.float32), axis=0).astype(jnp.bfloat16)
    copies = jnp.broadcast_to(piece[None], (Z,) + piece.shape)
    copies = lax.all_to_all(copies, "z", 0, 0, tiled=True)
    total = jnp.sum(copies.astype(jnp.float32), axis=0).astype(jnp.bfloat16)
    copies = jnp.broadcast_to(total[None], (YX,) + total.shape)
    return lax.all_to_all(copies, "yx", 0, 0, tiled=True).reshape(rows, columns)


def on_device(three_center, screen_mask, green_occ, green_virt):
    mu_dev, width, p_dev = three_center.shape
    blocks = screen_mask.shape[1]
    other = lax.ppermute(three_center, "col", [(0, 1), (1, 0)])
    keep = jnp.repeat(screen_mask, width // blocks, axis=1).astype(jnp.bfloat16)[:, :, None]
    mine = three_center * keep
    occ_side = contract(green_occ, mine)
    here = pair(occ_side, contract(green_virt, mine))
    there = pair(occ_side, contract(green_virt, other * keep))
    first = lax.axis_index("col") == 0
    partial = jnp.where(
        first, jnp.concatenate([here, there], axis=1), jnp.concatenate([there, here], axis=1)
    )
    summed = sum_over_row(partial).astype(jnp.float32)
    return -summed / jnp.sqrt(jnp.float32(mu_dev * Z * YX * width))


def solution(mesh):
    fine = Mesh(mesh.devices.reshape(Z, YX, 2), ("z", "yx", "col"))
    return jax.shard_map(
        on_device,
        mesh=fine,
        in_specs=(P(("z", "yx"), None, "col"), P(("z", "yx"), None), P(), P()),
        out_specs=P("col", None),
        check_vma=False,
    )
```

time: 448 us -> 80.1 us (0.18)
  the two profiles are of different devices: /device:TPU:2 before, /device:TPU:8 now
where the time goes in v1:
time: 80.1 us; the launch traced here: 79.8 us
  blocking collectives  64.6 us (81%)
  matrix products  11 us (14%)
  starting transfers between devices  2.04 us (3%)
  other arithmetic  1.74 us (2%)
    all_to_all x1, blocking collectives, sum_over_row(): pieces = lax.all_to_all(pieces, 'yx', 0, 0, tiled=True)  25.2 us
    all_to_all x1, blocking collectives, sum_over_row(): copies = lax.all_to_all(copies, 'z', 0, 0, tiled=True)  23.8 us
    all_to_all x1, blocking collectives, sum_over_row(): return lax.all_to_all(copies, 'yx', 0, 0, tiled=True).reshape(rows, columns)  15.6 us
    dot_general x2, matrix products, pair(): jnp.einsum('msp,msq->pq', occ_side, virt_side, preferred_element_type=jnp...  6.49 us
    dot_general x1, matrix products, contract(): jnp.einsum('sn,mnp->msp', green, screened, preferred_element_type=jnp.flo...  4.49 us
    ppermute x1, starting transfers between devices, on_device(): other = lax.ppermute(three_center, 'col', [(0, 1), (1, 0)])  2.04 us
  transfers between devices with their start and end apart: 1, of which 0 were waited for; matrix products, arithmetic and copies ran while one was open for 11% of the time, Pallas kernels for 0%

profile of v1, /device:TPU:8, one launch (start us, length us, event | category | flops | bytes accessed | tf_op | source)
XLA Modules:
  0.0 79.8 jit_solution(10664090768512716147)
XLA Ops:
  0.0 0.0 copy-start
  0.0 2.0 %collective-permute-start = (bf16[32,128,256]{2,1,0:T(8,128)(2,1)}, bf16[32,128,256]{2,1,0:T(8,128)(2,1)}, u32[]{:S(2)}, u32[]{:S(2)}) collective-permute-start(bf16[32,128,256]{2,1,0:T(8,128)(2,1)} %param.4), channel_id=1, source_target_pairs={{0,1},{1,0},{2,3},{3,2},{4,5},{5,4},{6,7},{7,6},{8,9},{9,8},{10,11... | collective-permute-start | bytes 6291464 | tf_op jit(solution)/shard_map/ppermute | solution.py:34
  2.1 0.7 convert_element_type.41
  2.7 0.1 copy.7
  2.8 0.1 broadcast_in_dim.6
  3.0 0.1 convert_element_type.42
  3.0 0.0 copy-done
  3.0 0.0 copy-start.1
  3.0 0.0 copy-start.2
  3.1 4.5 %convolution_convert_fusion = bf16[32,256,128]{2,1,0:T(8,128)(2,1)} fusion(bf16[32,128,256]{2,1,0:T(8,128)(2,1)} %param.4, bf16[32,128]{1,0:T(8,128)(2,1)S(1)} %convert_element_type.42, bf16[128,128]{1,0:T(8,128)(2,1)S(1)} %copy-done), kind=kOutput, calls=%fused_computation.11 | convolution fusion | flops 270532608 | bytes 4235264 | tf_op jit(solution)/shard_map/sn,mnp->msp/dot_general | solution.py:10
  7.6 0.0 copy-done.1
  7.6 0.0 copy-done.2
  7.6 2.9 %fusion.17 = bf16[32,8,256]{2,1,0:T(8,128)(2,1)S(1)} fusion(bf16[32,128,256]{2,1,0:T(8,128)(2,1)S(1)} %copy-done.1, bf16[32,256,128]{2,1,0:T(8,128)(2,1)} %convolution_convert_fusion, bf16[32,128]{1,0:T(8,128)(2,1)S(1)} %convert_element_type.42, bf16[128,128]{1,0:T(8,128)(2,1)S(1)} %copy-done.2), kind=kOutput, calls=%fused_computation.14 | convolution fusion | flops 810549248 | bytes 4366336 | tf_op jit(solution)/shard_map/msp,msq->pq/dot_general | solution.py:16
  10.5 0.0 collective-permute-done
  10.5 3.6 %fusion.24 = bf16[32,8,256]{2,1,0:T(8,128)(2,1)S(1)} fusion(bf16[32,128,256]{2,1,0:T(8,128)(2,1)} %collective-permute-done, bf16[32,256,128]{2,1,0:T(8,128)(2,1)} %convolution_convert_fusion, bf16[32,128]{1,0:T(8,128)(2,1)S(1)} %convert_element_type.42, bf16[128,128]{1,0:T(8,128)(2,1)S(1)} %copy-done.2), kind=kOutput, calls=%fused_computation.15 | convolution fusion | flops 810549248 | bytes 4366336 | tf_op jit(solution)/shard_map/msp,msq->pq/dot_general | solution.py:16
  14.1 0.1 fusion.36
  14.2 25.2 %all_to_all.15 = bf16[32,8,512]{2,1,0:T(8,128)(2,1)S(1)} all-to-all(bf16[32,8,512]{2,1,0:T(8,128)(2,1)S(1)} %fusion.36), channel_id=1, replica_groups=mesh['z'=12,'yx'=32,'col'=2] {'yx'}, dimensions={0} | all-to-all | bytes 524288 | tf_op jit(solution)/shard_map/all_to_all | solution.py:22
  39.4 0.1 reduce_sum.24
  39.5 23.8 %all_to_all.16 = bf16[12,8,512]{2,1,0:T(8,128)(2,1)S(1)} all-to-all(bf16[12,8,512]{2,1,0:T(8,128)(2,1)S(1)} %broadcast_in_dim.7), channel_id=1, replica_groups=mesh['z'=12,'yx'=32,'col'=2] {'z'}, dimensions={0} | all-to-all | bytes 196608 | tf_op jit(solution)/shard_map/all_to_all | solution.py:25
  63.3 15.6 %all_to_all.17 = bf16[32,8,512]{2,1,0:T(8,128)(2,1)S(1)} all-to-all(bf16[32,8,512]{2,1,0:T(8,128)(2,1)S(1)} %broadcast_in_dim.8), channel_id=1, replica_groups=mesh['z'=12,'yx'=32,'col'=2] {'yx'}, dimensions={0} | all-to-all | bytes 524288 | tf_op jit(solution)/shard_map/all_to_all | solution.py:28
  78.9 0.9 %multiply_bitcast_fusion = f32[256,512]{1,0:T(8,128)} fusion(bf16[32,8,512]{2,1,0:T(8,128)(2,1)S(1)} %all_to_all.17), kind=kLoop, calls=%fused_computation.21 | loop fusion | flops 393216 | bytes 786432 | tf_op jit(solution)/shard_map/div | solution.py:45
  (3 shorter events, 0.1 us)
Async XLA Ops:
  0.0 3.0 %copy-start = (bf16[128,128]{1,0:T(8,128)(2,1)S(1)}, bf16[128,128]{1,0:T(8,128)(2,1)}, u32[]{:S(2)}) copy-start(bf16[128,128]{1,0:T(8,128)(2,1)} %param.6) | copy-start | bytes 98308
  0.0 10.5 %collective-permute-start = (bf16[32,128,256]{2,1,0:T(8,128)(2,1)}, bf16[32,128,256]{2,1,0:T(8,128)(2,1)}, u32[]{:S(2)}, u32[]{:S(2)}) collective-permute-start(bf16[32,128,256]{2,1,0:T(8,128)(2,1)} %param.4), channel_id=1, source_target_pairs={{0,1},{1,0},{2,3},{3,2},{4,5},{5,4},{6,7},{7,6},{8,9},{9,8},{10,11... | collective-permute-start | bytes 6291464 | tf_op jit(solution)/shard_map/ppermute | solution.py:34
  3.0 4.5 %copy-start.1 = (bf16[32,128,256]{2,1,0:T(8,128)(2,1)S(1)}, bf16[32,128,256]{2,1,0:T(8,128)(2,1)}, u32[]{:S(2)}) copy-start(bf16[32,128,256]{2,1,0:T(8,128)(2,1)} %param.4) | copy-start | bytes 6291460
  3.0 4.5 %copy-start.2 = (bf16[128,128]{1,0:T(8,128)(2,1)S(1)}, bf16[128,128]{1,0:T(8,128)(2,1)}, u32[]{:S(2)}) copy-start(bf16[128,128]{1,0:T(8,128)(2,1)} %param.7) | copy-start | bytes 98308

commit v2 on v1

v2 whole, which is shorter than its diff:
```python
import jax
import jax.numpy as jnp
from jax import lax
from jax.experimental import pallas as pl
from jax.experimental.pallas import tpu as pltpu
from jax.sharding import Mesh, PartitionSpec as P

Z, YX = 12, 32
CHUNKS = 4
VMEM = pl.BlockSpec(memory_space=pltpu.VMEM)
SMEM = pl.BlockSpec(memory_space=pltpu.SMEM)
HBM = pl.BlockSpec(memory_space=pltpu.HBM)
PARAMS = pltpu.CompilerParams(vmem_limit_bytes=32 * 2**20)


def masked(x, keep_ref, m):
    half = x.shape[0] // 2
    zero = jnp.zeros((half, x.shape[1]), x.dtype)
    return jnp.concatenate(
        [
            jnp.where(keep_ref[0, m] != 0, x[:half], zero),
            jnp.where(keep_ref[1, m] != 0, x[half:], zero),
        ],
        axis=0,
    )


def local_kernel(keep_hbm, occ_hbm, virt_hbm, x_hbm, occ_ref, here_ref, keep, green, x, virt, sems):
    count, width, _ = x.shape
    per_chunk = count // CHUNKS

    def chunk(c):
        part = pl.ds(c * per_chunk, per_chunk)
        return pltpu.make_async_copy(x_hbm.at[part], x.at[part], sems.at[c])

    small = [
        pltpu.make_async_copy(keep_hbm, keep, sems.at[CHUNKS]),
        pltpu.make_async_copy(occ_hbm, green.at[pl.ds(0, width)], sems.at[CHUNKS + 1]),
        pltpu.make_async_copy(virt_hbm, green.at[pl.ds(width, width)], sems.at[CHUNKS + 2]),
    ]
    for copy in small:
        copy.start()
    for c in range(CHUNKS):
        chunk(c).start()
    for copy in small:
        copy.wait()
    for c in range(CHUNKS):
        chunk(c).wait()
        for m in range(c * per_chunk, (c + 1) * per_chunk):
            both = jnp.dot(green[...], masked(x[m], keep, m), preferred_element_type=jnp.float32)
            both = both.astype(jnp.bfloat16)
            occ_ref[:, m * width : (m + 1) * width] = both[:width].T
            virt[m * width : (m + 1) * width, :] = both[width:]
    here = jnp.dot(occ_ref[...], virt[...], preferred_element_type=jnp.float32)
    here_ref[...] = here.astype(jnp.bfloat16)


def local_part(three_center, keep, green_occ, green_virt):
    count, width, own = three_center.shape
    args = (keep, green_occ, green_virt, three_center)
    return pl.pallas_call(
        local_kernel,
        in_specs=[HBM] * 4,
        out_specs=[VMEM, VMEM],
        out_shape=[
            jax.ShapeDtypeStruct((own, count * width), jnp.bfloat16),
            jax.ShapeDtypeStruct((own, own), jnp.bfloat16),
        ],
        scratch_shapes=[
            pltpu.SMEM(keep.shape, keep.dtype),
            pltpu.VMEM((2 * width, width), jnp.bfloat16),
            pltpu.VMEM(three_center.shape, jnp.bfloat16),
            pltpu.VMEM((count * width, own), jnp.bfloat16),
            pltpu.SemaphoreType.DMA((CHUNKS + 3,)),
        ],
        compiler_params=PARAMS,
    )(*[pltpu.with_memory_space_constraint(a, pltpu.HBM) for a in args])


def remote_kernel(keep, first_ref, green_ref, x_ref, occ_ref, here_ref, out_ref, virt):
    count, width, own = x_ref.shape
    green = green_ref[...]
    for m in range(count):
        side = jnp.dot(green, masked(x_ref[m], keep, m), preferred_element_type=jnp.float32)
        virt[m * width : (m + 1) * width, :] = side.astype(jnp.bfloat16)
    there = jnp.dot(occ_ref[...], virt[...], preferred_element_type=jnp.float32)
    there = there.astype(jnp.bfloat16)
    here = here_ref[...]
    first = first_ref[0] != 0
    out_ref[:, :own] = jnp.where(first, here, there)
    out_ref[:, own:] = jnp.where(first, there, here)


def remote_part(other, keep, first, green_virt, occ_side, here):
    count, width, own = other.shape
    return pl.pallas_call(
        remote_kernel,
        in_specs=[SMEM, SMEM, VMEM, VMEM, VMEM, VMEM],
        out_specs=VMEM,
        out_shape=jax.ShapeDtypeStruct((own, 2 * own), jnp.bfloat16),
        scratch_shapes=[pltpu.VMEM((count * width, own), jnp.bfloat16)],
        compiler_params=PARAMS,
    )(keep, first, green_virt, other, occ_side, here)


def sum_over_row(partial):
    rows, columns = partial.shape
    pieces = partial.reshape(YX, rows // YX, columns)
    pieces = lax.all_to_all(pieces, "yx", 0, 0, tiled=True)
    piece = jnp.sum(pieces.astype(jnp.float32), axis=0).astype(jnp.bfloat16)
    copies = jnp.broadcast_to(piece[None], (Z,) + piece.shape)
    copies = lax.all_to_all(copies, "z", 0, 0, tiled=True)
    total = jnp.sum(copies.astype(jnp.float32), axis=0).astype(jnp.bfloat16)
    copies = jnp.broadcast_to(total[None], (YX,) + total.shape)
    return lax.all_to_all(copies, "yx", 0, 0, tiled=True).reshape(rows, columns)


def on_device(three_center, screen_mask, green_occ, green_virt):
    mu_dev, width, _ = three_center.shape
    other = lax.ppermute(three_center, "col", [(0, 1), (1, 0)])
    keep = screen_mask.T
    occ_side, here = local_part(three_center, keep, green_occ, green_virt)
    first = (lax.axis_index("col") == 0).astype(jnp.int32).reshape(1)
    partial = remote_part(other, keep, first, green_virt, occ_side, here)
    summed = sum_over_row(partial).astype(jnp.float32)
    return -summed / jnp.sqrt(jnp.float32(mu_dev * Z * YX * width))


def solution(mesh):
    fine = Mesh(mesh.devices.reshape(Z, YX, 2), ("z", "yx", "col"))
    return jax.shard_map(
        on_device,
        mesh=fine,
        in_specs=(P(("z", "yx"), None, "col"), P(("z", "yx"), None), P(), P()),
        out_specs=P("col", None),
        check_vma=False,
    )
```

time: 80.1 us -> 74.6 us (0.931)
  matrix products: 11 us -> 0 us
  Pallas kernels: 0 us -> 6.67 us
  other arithmetic: 1.74 us -> 0.93 us
    dot_general x3 -> x0, matrix products: 11 us -> none  [the longest x2 6.49 us: pair(): jnp.einsum('msp,msq->pq', occ_side, virt_side, preferred_element_type=jnp...]
    pallas_call x0 -> x2, Pallas kernels: none -> 6.67 us  [the longest x1 4.57 us: local_part(): pl.pallas_call(local_kernel, in_specs=[HBM] * 4, out_specs=[VMEM, VMEM],...]
    convert_element_type x2 -> x0, other arithmetic: 0.81 us -> none  [the longest x1 0.68 us: on_device(): jnp.repeat(screen_mask, width // blocks, axis=1).astype(jnp.bfloat16)]
  transfers between devices with their start and end apart: 1 -> 1, of which waited for: 0 -> 0; matrix products, arithmetic and copies ran while one was open for 11% -> 0% of each run, Pallas kernels for 0% -> 6%
where the time goes in v2:
time: 74.6 us; the launch traced here: 74.3 us
  blocking collectives  64.6 us (87%)
  Pallas kernels  6.67 us (9%)
  starting transfers between devices  2.04 us (3%)
  other arithmetic  0.93 us (1%)
    all_to_all x1, blocking collectives, sum_over_row(): pieces = lax.all_to_all(pieces, 'yx', 0, 0, tiled=True)  25.2 us
    all_to_all x1, blocking collectives, sum_over_row(): copies = lax.all_to_all(copies, 'z', 0, 0, tiled=True)  23.8 us
    all_to_all x1, blocking collectives, sum_over_row(): return lax.all_to_all(copies, 'yx', 0, 0, tiled=True).reshape(rows, columns)  15.6 us
    pallas_call x1, Pallas kernels, local_part(): pl.pallas_call(local_kernel, in_specs=[HBM] * 4, out_specs=[VMEM, VMEM],...  4.57 us
    pallas_call x1, Pallas kernels, remote_part(): pl.pallas_call(remote_kernel, in_specs=[SMEM, SMEM, VMEM, VMEM, VMEM, VME...  2.1 us
    ppermute x1, starting transfers between devices, on_device(): other = lax.ppermute(three_center, 'col', [(0, 1), (1, 0)])  2.04 us
  transfers between devices with their start and end apart: 1, of which 0 were waited for; matrix products, arithmetic and copies ran while one was open for 0% of the time, Pallas kernels for 6%

profile of v2, /device:TPU:8, one launch (start us, length us, event | category | flops | bytes accessed | tf_op | source)
XLA Modules:
  0.0 74.3 jit_solution(5227747909407638152)
XLA Ops:
  0.0 0.0 copy-start
  0.0 0.0 copy-start.1
  0.0 2.0 %collective-permute-start = (bf16[32,128,256]{2,1,0:T(8,128)(2,1)}, bf16[32,128,256]{2,1,0:T(8,128)(2,1)S(1)}, u32[]{:S(2)}, u32[]{:S(2)}) collective-permute-start(bf16[32,128,256]{2,1,0:T(8,128)(2,1)} %x_hbm.1), channel_id=1, source_target_pairs={{0,1},{1,0},{2,3},{3,2},{4,5},{5,4},{6,7},{7,6},{8,9},{9,8},{10,11... | collective-permute-start | bytes 6291464 | tf_op jit(solution)/shard_map/ppermute | solution.py:120
  2.1 4.6 %shard_map.46 = (bf16[256,4096]{1,0:T(8,128)(2,1)S(1)}, bf16[256,256]{1,0:T(8,128)(2,1)S(1)}) custom-call(s32[2,32]{1,0:T(2,128)} %bitcast.6, bf16[128,128]{1,0:T(8,128)(2,1)} %occ_hbm.1, bf16[128,128]{1,0:T(8,128)(2,1)} %green_ref.1, bf16[32,128,256]{2,1,0:T(8,128)(2,1)} %x_hbm.1), custom_call_target="tpu_custom_call" | custom-call | tf_op jit(solution)/shard_map/pallas_call | solution.py:61
  6.6 0.0 collective-permute-done.x_ref
  6.6 0.0 copy-done
  6.7 0.0 copy-done.1
  6.7 2.1 %shard_map.47 = bf16[256,512]{1,0:T(8,128)(2,1)S(1)} custom-call(s32[2,32]{1,0:T(2,128)S(1)} %bitcast.7, s32[1]{0:T(128)} %bitcast.1.first_ref, bf16[128,128]{1,0:T(8,128)(2,1)S(1)} %copy-done, bf16[32,128,256]{2,1,0:T(8,128)(2,1)S(1)} %collective-permute-done.x_ref, bf16[256,4096]{1,0:T(8,128)(2,1)S(1)} %get-tuple-element.7.occ_ref, ...), custom_call_target="tpu_custom_call" | custom-call | tf_op jit(solution)/shard_map/pallas_call | solution.py:96
  8.8 25.2 %all_to_all.15 = bf16[32,8,512]{2,1,0:T(8,128)(2,1)S(1)} all-to-all(bf16[32,8,512]{2,1,0:T(8,128)(2,1)S(1)} %bitcast.5), channel_id=1, replica_groups=mesh['z'=12,'yx'=32,'col'=2] {'yx'}, dimensions={0} | all-to-all | bytes 524288 | tf_op jit(solution)/shard_map/all_to_all | solution.py:109
  34.0 0.1 reduce_sum.24
  34.1 23.8 %all_to_all.16 = bf16[12,8,512]{2,1,0:T(8,128)(2,1)S(1)} all-to-all(bf16[12,8,512]{2,1,0:T(8,128)(2,1)S(1)} %broadcast_in_dim.4), channel_id=1, replica_groups=mesh['z'=12,'yx'=32,'col'=2] {'z'}, dimensions={0} | all-to-all | bytes 196608 | tf_op jit(solution)/shard_map/all_to_all | solution.py:112
  57.9 15.6 %all_to_all.17 = bf16[32,8,512]{2,1,0:T(8,128)(2,1)S(1)} all-to-all(bf16[32,8,512]{2,1,0:T(8,128)(2,1)S(1)} %broadcast_in_dim.5), channel_id=1, replica_groups=mesh['z'=12,'yx'=32,'col'=2] {'yx'}, dimensions={0} | all-to-all | bytes 524288 | tf_op jit(solution)/shard_map/all_to_all | solution.py:115
  73.5 0.9 %multiply_bitcast_fusion = f32[256,512]{1,0:T(8,128)} fusion(bf16[32,8,512]{2,1,0:T(8,128)(2,1)S(1)} %all_to_all.17), kind=kLoop, calls=%fused_computation | loop fusion | flops 393216 | bytes 786432 | tf_op jit(solution)/shard_map/div | solution.py:126
  (3 shorter events, 0.1 us)
Async XLA Ops:
  0.0 6.6 %copy-start = (bf16[128,128]{1,0:T(8,128)(2,1)S(1)}, bf16[128,128]{1,0:T(8,128)(2,1)}, u32[]{:S(2)}) copy-start(bf16[128,128]{1,0:T(8,128)(2,1)} %green_ref.1) | copy-start | bytes 98308
  0.0 6.7 %copy-start.1 = (s32[32,2]{0,1:T(2,128)S(1)}, s32[32,2]{0,1:T(2,128)}, u32[]{:S(2)}) copy-start(s32[32,2]{0,1:T(2,128)} %param.5) | copy-start | bytes 772
  0.0 6.6 %collective-permute-start = (bf16[32,128,256]{2,1,0:T(8,128)(2,1)}, bf16[32,128,256]{2,1,0:T(8,128)(2,1)S(1)}, u32[]{:S(2)}, u32[]{:S(2)}) collective-permute-start(bf16[32,128,256]{2,1,0:T(8,128)(2,1)} %x_hbm.1), channel_id=1, source_target_pairs={{0,1},{1,0},{2,3},{3,2},{4,5},{5,4},{6,7},{7,6},{8,9},{9,8},{10,11... | collective-permute-start | bytes 6291464 | tf_op jit(solution)/shard_map/ppermute | solution.py:120

commit v3 on v2

v3 whole, which is shorter than its diff:
```python
import jax
import jax.numpy as jnp
from jax import lax
from jax.experimental import pallas as pl
from jax.experimental.pallas import tpu as pltpu
from jax.sharding import Mesh, PartitionSpec as P

Z, YX = 12, 32
CHUNKS = 4
VMEM = pl.BlockSpec(memory_space=pltpu.VMEM)
HBM = pl.BlockSpec(memory_space=pltpu.HBM)
PARAMS = pltpu.CompilerParams(vmem_limit_bytes=32 * 2**20)


def transposed_dot(a, b):
    return lax.dot_general(a, b, (((0,), (0,)), ((), ())), preferred_element_type=jnp.float32)


def local_kernel(
    keep_hbm, occ_hbm, virt_hbm, x_hbm, occ_ref, here_ref, kept_ref,
    keep, green, table, x, virt, sems,
):
    count, width, _ = x.shape
    per_chunk = count // CHUNKS

    def chunk(c):
        part = pl.ds(c * per_chunk, per_chunk)
        return pltpu.make_async_copy(x_hbm.at[part], x.at[part], sems.at[c])

    small = [
        pltpu.make_async_copy(keep_hbm, keep, sems.at[CHUNKS]),
        pltpu.make_async_copy(occ_hbm, green.at[pl.ds(0, width)], sems.at[CHUNKS + 1]),
        pltpu.make_async_copy(virt_hbm, green.at[pl.ds(width, width)], sems.at[CHUNKS + 2]),
    ]
    for copy in small:
        copy.start()
    for c in range(CHUNKS):
        chunk(c).start()
    for copy in small:
        copy.wait()
    whole = green[...]
    zero = jnp.zeros_like(whole)
    lower = lax.broadcasted_iota(jnp.int32, whole.shape, 1) < width // 2
    table[0] = zero
    table[1] = jnp.where(lower, zero, whole)
    table[2] = jnp.where(lower, whole, zero)
    table[3] = whole
    here = jnp.zeros(here_ref.shape, jnp.float32)
    for c in range(CHUNKS):
        chunk(c).wait()
        for m in range(c * per_chunk, (c + 1) * per_chunk):
            rows = pl.ds(m * width, width)
            which = jnp.where(keep[0, m] != 0, 2, 0) + jnp.where(keep[1, m] != 0, 1, 0)
            kept = table[which]
            kept_ref[m] = kept[width:]
            both = jnp.dot(kept, x[m], preferred_element_type=jnp.float32).astype(jnp.bfloat16)
            occ_ref[rows, :] = both[:width]
            virt[rows, :] = both[width:]
        rows = pl.ds(c * per_chunk * width, per_chunk * width)
        here = here + transposed_dot(occ_ref[rows, :], virt[rows, :])
    here_ref[...] = here.astype(jnp.bfloat16)


def local_part(three_center, keep, green_occ, green_virt):
    count, width, own = three_center.shape
    args = (keep, green_occ, green_virt, three_center)
    return pl.pallas_call(
        local_kernel,
        in_specs=[HBM] * 4,
        out_specs=[VMEM] * 3,
        out_shape=[
            jax.ShapeDtypeStruct((count * width, own), jnp.bfloat16),
            jax.ShapeDtypeStruct((own, own), jnp.bfloat16),
            jax.ShapeDtypeStruct((count, width, width), jnp.bfloat16),
        ],
        scratch_shapes=[
            pltpu.SMEM(keep.shape, keep.dtype),
            pltpu.VMEM((2 * width, width), jnp.bfloat16),
            pltpu.VMEM((4, 2 * width, width), jnp.bfloat16),
            pltpu.VMEM(three_center.shape, jnp.bfloat16),
            pltpu.VMEM((count * width, own), jnp.bfloat16),
            pltpu.SemaphoreType.DMA((CHUNKS + 3,)),
        ],
        compiler_params=PARAMS,
    )(*[pltpu.with_memory_space_constraint(a, pltpu.HBM) for a in args])


def remote_kernel(kept_ref, x_ref, occ_ref, here_ref, out_ref, virt):
    count, width, own = x_ref.shape
    for m in range(count):
        side = jnp.dot(kept_ref[m], x_ref[m], preferred_element_type=jnp.float32)
        virt[m * width : (m + 1) * width, :] = side.astype(jnp.bfloat16)
    out_ref[:, :own] = here_ref[...]
    out_ref[:, own:] = transposed_dot(occ_ref[...], virt[...]).astype(jnp.bfloat16)


def remote_part(other, kept, occ_side, here):
    count, width, own = other.shape
    return pl.pallas_call(
        remote_kernel,
        in_specs=[VMEM] * 4,
        out_specs=VMEM,
        out_shape=jax.ShapeDtypeStruct((own, 2 * own), jnp.bfloat16),
        scratch_shapes=[pltpu.VMEM((count * width, own), jnp.bfloat16)],
        compiler_params=PARAMS,
    )(kept, other, occ_side, here)


def sum_over_row(partial):
    rows, columns = partial.shape
    pieces = partial.reshape(YX, rows // YX, columns)
    pieces = lax.all_to_all(pieces, "yx", 0, 0, tiled=True)
    piece = jnp.sum(pieces.astype(jnp.float32), axis=0).astype(jnp.bfloat16)
    copies = jnp.broadcast_to(piece[None], (Z,) + piece.shape)
    copies = lax.all_to_all(copies, "z", 0, 0, tiled=True)
    total = jnp.sum(copies.astype(jnp.float32), axis=0).astype(jnp.bfloat16)
    copies = jnp.broadcast_to(total[None], (YX,) + total.shape)
    return lax.all_to_all(copies, "yx", 0, 0, tiled=True).reshape(rows, columns)


def on_device(three_center, screen_mask, green_occ, green_virt):
    mu_dev, width, own = three_center.shape
    other = lax.ppermute(three_center, "col", [(0, 1), (1, 0)])
    occ_side, here, kept = local_part(three_center, screen_mask.T, green_occ, green_virt)
    partial = remote_part(other, kept, occ_side, here)
    summed = sum_over_row(partial)
    swapped = jnp.concatenate([summed[:, own:], summed[:, :own]], axis=1)
    ordered = jnp.where(lax.axis_index("col") == 0, summed, swapped).astype(jnp.float32)
    return -ordered / jnp.sqrt(jnp.float32(mu_dev * Z * YX * width))


def solution(mesh):
    fine = Mesh(mesh.devices.reshape(Z, YX, 2), ("z", "yx", "col"))
    return jax.shard_map(
        on_device,
        mesh=fine,
        in_specs=(P(("z", "yx"), None, "col"), P(("z", "yx"), None), P(), P()),
        out_specs=P("col", None),
        check_vma=False,
    )
```

time: 74.6 us -> 74 us (level)
  blocking collectives: 64.6 us -> 49.1 us
  waiting for transfers between devices: 0.01 us -> 11.1 us
  starting transfers between devices: 2.04 us -> 6.52 us
  Pallas kernels: 6.67 us -> 5.28 us
    all_to_all x1 -> x0, blocking collectives: 15.6 us -> none  [sum_over_row(): return lax.all_to_all(copies, 'yx', 0, 0, tiled=True).reshape(rows, columns)]
    all_to_all x0 -> x1, waiting for transfers between devices: none -> 10.8 us  [sum_over_row(): return lax.all_to_all(copies, 'yx', 0, 0, tiled=True).reshape(rows, columns)]
    all_to_all x0 -> x1, starting transfers between devices: none -> 4.62 us  [sum_over_row(): return lax.all_to_all(copies, 'yx', 0, 0, tiled=True).reshape(rows, columns)]
    pallas_call x2, Pallas kernels: 6.67 us -> 5.28 us  [the longest x1 4.02 us: local_part(): pl.pallas_call(local_kernel, in_specs=[HBM] * 4, out_specs=[VMEM] * 3, ou...]
  transfers between devices with their start and end apart: 1 -> 2, of which waited for: 0 -> 2; matrix products, arithmetic and copies ran while one was open for 0% -> 0% of each run, Pallas kernels for 6% -> 5%
where the time goes in v3:
time: 74 us; the launch traced here: 73.7 us
  blocking collectives  49.1 us (66%)
  waiting for transfers between devices  11.1 us (15%)
  starting transfers between devices  6.52 us (9%)
  Pallas kernels  5.28 us (7%)
  other arithmetic  0.95 us (1%)
  local copies, waits for them, and re-layouts  0.75 us (1%)
    all_to_all x1, blocking collectives, sum_over_row(): pieces = lax.all_to_all(pieces, 'yx', 0, 0, tiled=True)  25 us
    all_to_all x1, blocking collectives, sum_over_row(): copies = lax.all_to_all(copies, 'z', 0, 0, tiled=True)  24.1 us
    all_to_all x1, waiting for transfers between devices, sum_over_row(): return lax.all_to_all(copies, 'yx', 0, 0, tiled=True).reshape(rows, columns)  10.8 us
    all_to_all x1, starting transfers between devices, sum_over_row(): return lax.all_to_all(copies, 'yx', 0, 0, tiled=True).reshape(rows, columns)  4.62 us
    pallas_call x1, Pallas kernels, local_part(): pl.pallas_call(local_kernel, in_specs=[HBM] * 4, out_specs=[VMEM] * 3, ou...  4.02 us
    ppermute x1, starting transfers between devices, on_device(): other = lax.ppermute(three_center, 'col', [(0, 1), (1, 0)])  1.91 us
  transfers between devices with their start and end apart: 2, of which 2 were waited for; matrix products, arithmetic and copies ran while one was open for 0% of the time, Pallas kernels for 5%

profile of v3, /device:TPU:8, one launch (start us, length us, event | category | flops | bytes accessed | tf_op | source)
XLA Modules:
  0.0 73.7 jit_solution(9702113700739670072)
XLA Ops:
  0.0 1.9 %collective-permute-start = (bf16[32,128,256]{2,1,0:T(8,128)(2,1)}, bf16[32,128,256]{2,1,0:T(8,128)(2,1)S(1)}, u32[]{:S(2)}, u32[]{:S(2)}) collective-permute-start(bf16[32,128,256]{2,1,0:T(8,128)(2,1)} %x_hbm.1), channel_id=1, source_target_pairs={{0,1},{1,0},{2,3},{3,2},{4,5},{5,4},{6,7},{7,6},{8,9},{9,8},{10,11... | collective-permute-start | bytes 6291464 | tf_op jit(solution)/shard_map/ppermute | solution.py:123
  1.9 4.0 %shard_map.46 = (bf16[4096,256]{1,0:T(8,128)(2,1)S(1)}, bf16[256,256]{1,0:T(8,128)(2,1)S(1)}, bf16[32,128,128]{2,1,0:T(8,128)(2,1)S(1)}) custom-call(s32[2,32]{1,0:T(2,128)} %bitcast.6, bf16[128,128]{1,0:T(8,128)(2,1)} %occ_hbm.1, bf16[128,128]{1,0:T(8,128)(2,1)} %virt_hbm.1, bf16[32,128,256]{2,1,0:T(8,128)(2,1)} %x_hbm.1), custom_call_target="tpu_custom_call" | custom-call | tf_op jit(solution)/shard_map/pallas_call | solution.py:67
  5.9 0.3 collective-permute-done.x_ref
  6.3 1.3 %shard_map.47 = bf16[256,512]{1,0:T(8,128)(2,1)S(1)} custom-call(bf16[32,128,128]{2,1,0:T(8,128)(2,1)S(1)} %get-tuple-element.8.kept_ref, bf16[32,128,256]{2,1,0:T(8,128)(2,1)S(1)} %collective-permute-done.x_ref, bf16[4096,256]{1,0:T(8,128)(2,1)S(1)} %get-tuple-element.9.occ_ref, bf16[256,256]{1,0:T(8,128)(2,1)S(1)} %get-tuple-element.10.here_ref), custom_call_target="tpu_custom_call" | custom-call | tf_op jit(solution)/shard_map/pallas_call | solution.py:99
  7.5 25.0 %all_to_all.15 = bf16[32,8,512]{2,1,0:T(8,128)(2,1)S(1)} all-to-all(bf16[32,8,512]{2,1,0:T(8,128)(2,1)S(1)} %bitcast.4), channel_id=1, replica_groups=mesh['z'=12,'yx'=32,'col'=2] {'yx'}, dimensions={0} | all-to-all | bytes 524288 | tf_op jit(solution)/shard_map/all_to_all | solution.py:112
  32.5 0.1 reduce_sum.24
  32.6 24.1 %all_to_all.16 = bf16[12,8,512]{2,1,0:T(8,128)(2,1)S(1)} all-to-all(bf16[12,8,512]{2,1,0:T(8,128)(2,1)S(1)} %broadcast_in_dim.4), channel_id=1, replica_groups=mesh['z'=12,'yx'=32,'col'=2] {'z'}, dimensions={0} | all-to-all | bytes 196608 | tf_op jit(solution)/shard_map/all_to_all | solution.py:115
  56.7 0.7 broadcast_in_dim.5
  57.4 4.6 %all-to-all-start.2 = ((bf16[32,8,512]{2,1,0:T(8,128)(2,1)}), bf16[32,8,512]{2,1,0:T(8,128)(2,1)S(1)}, u32[]{:S(2)}, u32[]{:S(2)}) async-start(bf16[32,8,512]{2,1,0:T(8,128)(2,1)} %broadcast_in_dim.5), calls=%async_computation.2 | async-start | bytes 524288 | tf_op jit(solution)/shard_map/all_to_all | solution.py:118
  62.0 10.8 %all-to-all-done.2 = bf16[32,8,512]{2,1,0:T(8,128)(2,1)S(1)} async-done(((bf16[32,8,512]{2,1,0:T(8,128)(2,1)}), bf16[32,8,512]{2,1,0:T(8,128)(2,1)S(1)}, u32[]{:S(2)}, u32[]{:S(2)}) %all-to-all-start.2) | async-done | bytes 262176 | tf_op jit(solution)/shard_map/all_to_all | solution.py:118
  72.8 0.9 %negate_multiply_fusion = f32[256,512]{1,0:T(8,128)} fusion(bf16[256,256]{1,0:T(8,128)(2,1)S(1)} %get-tuple-element.12, bf16[256,256]{1,0:T(8,128)(2,1)S(1)} %get-tuple-element.11, pred[]{:T(512)S(6)} %eq.3, bf16[32,8,512]{2,1,0:T(8,128)(2,1)S(1)} %all-to-all-done.2), kind=kLoop, calls=%fused_computation | loop fusion | flops 1048576 | bytes 1048577 | tf_op jit(solution)/shard_map/div | solution.py:129
  (3 shorter events, 0.0 us)
Async XLA Ops:
  0.0 6.3 %collective-permute-start = (bf16[32,128,256]{2,1,0:T(8,128)(2,1)}, bf16[32,128,256]{2,1,0:T(8,128)(2,1)S(1)}, u32[]{:S(2)}, u32[]{:S(2)}) collective-permute-start(bf16[32,128,256]{2,1,0:T(8,128)(2,1)} %x_hbm.1), channel_id=1, source_target_pairs={{0,1},{1,0},{2,3},{3,2},{4,5},{5,4},{6,7},{7,6},{8,9},{9,8},{10,11... | collective-permute-start | bytes 6291464 | tf_op jit(solution)/shard_map/ppermute | solution.py:123
  57.4 15.4 %all-to-all-start.2 = ((bf16[32,8,512]{2,1,0:T(8,128)(2,1)}), bf16[32,8,512]{2,1,0:T(8,128)(2,1)S(1)}, u32[]{:S(2)}, u32[]{:S(2)}) async-start(bf16[32,8,512]{2,1,0:T(8,128)(2,1)} %broadcast_in_dim.5), calls=%async_computation.2 | async-start | bytes 524288 | tf_op jit(solution)/shard_map/all_to_all | solution.py:118

commit v4 on v3

--- a/solution.py
+++ b/solution.py
@@ -90,8 +90,11 @@
     for m in range(count):
         side = jnp.dot(kept_ref[m], x_ref[m], preferred_element_type=jnp.float32)
         virt[m * width : (m + 1) * width, :] = side.astype(jnp.bfloat16)
-    out_ref[:, :own] = here_ref[...]
-    out_ref[:, own:] = transposed_dot(occ_ref[...], virt[...]).astype(jnp.bfloat16)
+    there = transposed_dot(occ_ref[...], virt[...]).astype(jnp.bfloat16)
+    here = here_ref[...]
+    first = lax.axis_index("col") == 0
+    out_ref[:, :own] = jnp.where(first, here, there)
+    out_ref[:, own:] = jnp.where(first, there, here)
 
 
 def remote_part(other, kept, occ_side, here):
@@ -119,14 +122,12 @@
 
 
 def on_device(three_center, screen_mask, green_occ, green_virt):
-    mu_dev, width, own = three_center.shape
+    mu_dev, width, _ = three_center.shape
     other = lax.ppermute(three_center, "col", [(0, 1), (1, 0)])
     occ_side, here, kept = local_part(three_center, screen_mask.T, green_occ, green_virt)
     partial = remote_part(other, kept, occ_side, here)
-    summed = sum_over_row(partial)
-    swapped = jnp.concatenate([summed[:, own:], summed[:, :own]], axis=1)
-    ordered = jnp.where(lax.axis_index("col") == 0, summed, swapped).astype(jnp.float32)
-    return -ordered / jnp.sqrt(jnp.float32(mu_dev * Z * YX * width))
+    summed = sum_over_row(partial).astype(jnp.float32)
+    return -summed / jnp.sqrt(jnp.float32(mu_dev * Z * YX * width))
 
 
 def solution(mesh):

time: 74 us -> 73 us (0.986)
  blocking collectives: 49.1 us -> 64.3 us
  waiting for transfers between devices: 11.1 us -> 0.31 us
  starting transfers between devices: 6.52 us -> 1.91 us
    all_to_all x0 -> x1, blocking collectives: none -> 15.2 us  [sum_over_row(): return lax.all_to_all(copies, 'yx', 0, 0, tiled=True).reshape(rows, columns)]
    all_to_all x1 -> x0, waiting for transfers between devices: 10.8 us -> none  [sum_over_row(): return lax.all_to_all(copies, 'yx', 0, 0, tiled=True).reshape(rows, columns)]
    all_to_all x1 -> x0, starting transfers between devices: 4.62 us -> none  [sum_over_row(): return lax.all_to_all(copies, 'yx', 0, 0, tiled=True).reshape(rows, columns)]
  transfers between devices with their start and end apart: 2 -> 1, of which waited for: 2 -> 1; matrix products, arithmetic and copies ran while one was open for 0% -> 0% of each run, Pallas kernels for 5% -> 6%
where the time goes in v4:
time: 73 us; the launch traced here: 72.8 us
  blocking collectives  64.3 us (88%)
  Pallas kernels  5.28 us (7%)
  starting transfers between devices  1.91 us (3%)
  other arithmetic  0.93 us (1%)
    all_to_all x1, blocking collectives, sum_over_row(): pieces = lax.all_to_all(pieces, 'yx', 0, 0, tiled=True)  25 us
    all_to_all x1, blocking collectives, sum_over_row(): copies = lax.all_to_all(copies, 'z', 0, 0, tiled=True)  24.1 us
    all_to_all x1, blocking collectives, sum_over_row(): return lax.all_to_all(copies, 'yx', 0, 0, tiled=True).reshape(rows, columns)  15.2 us
    pallas_call x1, Pallas kernels, local_part(): pl.pallas_call(local_kernel, in_specs=[HBM] * 4, out_specs=[VMEM] * 3, ou...  4.02 us
    ppermute x1, starting transfers between devices, on_device(): other = lax.ppermute(three_center, 'col', [(0, 1), (1, 0)])  1.91 us
  transfers between devices with their start and end apart: 1, of which 1 were waited for; matrix products, arithmetic and copies ran while one was open for 0% of the time, Pallas kernels for 6%

profile of v4, /device:TPU:8, one launch (start us, length us, event | category | flops | bytes accessed | tf_op | source)
XLA Modules:
  0.0 72.8 jit_solution(1057569402941324187)
XLA Ops:
  0.0 1.9 %collective-permute-start = (bf16[32,128,256]{2,1,0:T(8,128)(2,1)}, bf16[32,128,256]{2,1,0:T(8,128)(2,1)S(1)}, u32[]{:S(2)}, u32[]{:S(2)}) collective-permute-start(bf16[32,128,256]{2,1,0:T(8,128)(2,1)} %x_hbm.1), channel_id=1, source_target_pairs={{0,1},{1,0},{2,3},{3,2},{4,5},{5,4},{6,7},{7,6},{8,9},{9,8},{10,11... | collective-permute-start | bytes 6291464 | tf_op jit(solution)/shard_map/ppermute | solution.py:126
  1.9 4.0 %shard_map.46 = (bf16[4096,256]{1,0:T(8,128)(2,1)S(1)}, bf16[256,256]{1,0:T(8,128)(2,1)S(1)}, bf16[32,128,128]{2,1,0:T(8,128)(2,1)S(1)}) custom-call(s32[2,32]{1,0:T(2,128)} %bitcast.5, bf16[128,128]{1,0:T(8,128)(2,1)} %occ_hbm.1, bf16[128,128]{1,0:T(8,128)(2,1)} %virt_hbm.1, bf16[32,128,256]{2,1,0:T(8,128)(2,1)} %x_hbm.1), custom_call_target="tpu_custom_call" | custom-call | tf_op jit(solution)/shard_map/pallas_call | solution.py:67
  5.9 0.3 collective-permute-done.x_ref
  6.3 1.3 %shard_map.47 = bf16[256,512]{1,0:T(8,128)(2,1)S(1)} custom-call(bf16[32,128,128]{2,1,0:T(8,128)(2,1)S(1)} %get-tuple-element.8.kept_ref, bf16[32,128,256]{2,1,0:T(8,128)(2,1)S(1)} %collective-permute-done.x_ref, bf16[4096,256]{1,0:T(8,128)(2,1)S(1)} %get-tuple-element.9.occ_ref, bf16[256,256]{1,0:T(8,128)(2,1)S(1)} %get-tuple-element.10.here_ref), custom_call_target="tpu_custom_call" | custom-call | tf_op jit(solution)/shard_map/pallas_call | solution.py:102
  7.5 25.0 %all_to_all.15 = bf16[32,8,512]{2,1,0:T(8,128)(2,1)S(1)} all-to-all(bf16[32,8,512]{2,1,0:T(8,128)(2,1)S(1)} %bitcast.4), channel_id=1, replica_groups=mesh['z'=12,'yx'=32,'col'=2] {'yx'}, dimensions={0} | all-to-all | bytes 524288 | tf_op jit(solution)/shard_map/all_to_all | solution.py:115
  32.5 0.1 reduce_sum.24
  32.6 24.1 %all_to_all.16 = bf16[12,8,512]{2,1,0:T(8,128)(2,1)S(1)} all-to-all(bf16[12,8,512]{2,1,0:T(8,128)(2,1)S(1)} %broadcast_in_dim.4), channel_id=1, replica_groups=mesh['z'=12,'yx'=32,'col'=2] {'z'}, dimensions={0} | all-to-all | bytes 196608 | tf_op jit(solution)/shard_map/all_to_all | solution.py:118
  56.7 15.2 %all_to_all.17 = bf16[32,8,512]{2,1,0:T(8,128)(2,1)S(1)} all-to-all(bf16[32,8,512]{2,1,0:T(8,128)(2,1)S(1)} %broadcast_in_dim.5), channel_id=1, replica_groups=mesh['z'=12,'yx'=32,'col'=2] {'yx'}, dimensions={0} | all-to-all | bytes 524288 | tf_op jit(solution)/shard_map/all_to_all | solution.py:121
  71.9 0.9 %multiply_bitcast_fusion = f32[256,512]{1,0:T(8,128)} fusion(bf16[32,8,512]{2,1,0:T(8,128)(2,1)S(1)} %all_to_all.17), kind=kLoop, calls=%fused_computation | loop fusion | flops 393216 | bytes 786432 | tf_op jit(solution)/shard_map/div | solution.py:130
  (3 shorter events, 0.1 us)
Async XLA Ops:
  0.0 6.3 %collective-permute-start = (bf16[32,128,256]{2,1,0:T(8,128)(2,1)}, bf16[32,128,256]{2,1,0:T(8,128)(2,1)S(1)}, u32[]{:S(2)}, u32[]{:S(2)}) collective-permute-start(bf16[32,128,256]{2,1,0:T(8,128)(2,1)} %x_hbm.1), channel_id=1, source_target_pairs={{0,1},{1,0},{2,3},{3,2},{4,5},{5,4},{6,7},{7,6},{8,9},{9,8},{10,11... | collective-permute-start | bytes 6291464 | tf_op jit(solution)/shard_map/ppermute | solution.py:126

commit v5 on v4

--- a/solution.py
+++ b/solution.py
@@ -5,7 +5,9 @@
 from jax.experimental.pallas import tpu as pltpu
 from jax.sharding import Mesh, PartitionSpec as P
 
-Z, YX = 12, 32
+CUTS = {"z_hi": 3, "z_lo": 4, "y_hi": 4, "y_lo": 2, "x": 4}
+NEAR, NEARS = ("y_lo", "x", "z_lo"), 32
+FAR, FARS = ("y_hi", "z_hi"), 12
 CHUNKS = 4
 VMEM = pl.BlockSpec(memory_space=pltpu.VMEM)
 HBM = pl.BlockSpec(memory_space=pltpu.HBM)
@@ -111,14 +113,14 @@
 
 def sum_over_row(partial):
     rows, columns = partial.shape
-    pieces = partial.reshape(YX, rows // YX, columns)
-    pieces = lax.all_to_all(pieces, "yx", 0, 0, tiled=True)
+    pieces = partial.reshape(NEARS, rows // NEARS, columns)
+    pieces = lax.all_to_all(pieces, NEAR, 0, 0, tiled=True)
     piece = jnp.sum(pieces.astype(jnp.float32), axis=0).astype(jnp.bfloat16)
-    copies = jnp.broadcast_to(piece[None], (Z,) + piece.shape)
-    copies = lax.all_to_all(copies, "z", 0, 0, tiled=True)
+    copies = jnp.broadcast_to(piece[None], (FARS,) + piece.shape)
+    copies = lax.all_to_all(copies, FAR, 0, 0, tiled=True)
     total = jnp.sum(copies.astype(jnp.float32), axis=0).astype(jnp.bfloat16)
-    copies = jnp.broadcast_to(total[None], (YX,) + total.shape)
-    return lax.all_to_all(copies, "yx", 0, 0, tiled=True).reshape(rows, columns)
+    copies = jnp.broadcast_to(total[None], (NEARS,) + total.shape)
+    return lax.all_to_all(copies, NEAR, 0, 0, tiled=True).reshape(rows, columns)
 
 
 def on_device(three_center, screen_mask, green_occ, green_virt):
@@ -127,15 +129,16 @@
     occ_side, here, kept = local_part(three_center, screen_mask.T, green_occ, green_virt)
     partial = remote_part(other, kept, occ_side, here)
     summed = sum_over_row(partial).astype(jnp.float32)
-    return -summed / jnp.sqrt(jnp.float32(mu_dev * Z * YX * width))
+    return -summed / jnp.sqrt(jnp.float32(mu_dev * NEARS * FARS * width))
 
 
 def solution(mesh):
-    fine = Mesh(mesh.devices.reshape(Z, YX, 2), ("z", "yx", "col"))
+    row = tuple(CUTS)
+    fine = Mesh(mesh.devices.reshape(*CUTS.values(), 2), row + ("col",))
     return jax.shard_map(
         on_device,
         mesh=fine,
-        in_specs=(P(("z", "yx"), None, "col"), P(("z", "yx"), None), P(), P()),
+        in_specs=(P(row, None, "col"), P(row, None), P(), P()),
         out_specs=P("col", None),
         check_vma=False,
     )

time: 73 us -> 73.4 us (level)
  no operation moved by 1% of the time
where the time goes in v5:
time: 73.4 us; the launch traced here: 73.1 us
  blocking collectives  64.6 us (88%)
  Pallas kernels  5.28 us (7%)
  starting transfers between devices  1.91 us (3%)
  other arithmetic  0.93 us (1%)
    all_to_all x1, blocking collectives, sum_over_row(): copies = lax.all_to_all(copies, FAR, 0, 0, tiled=True)  27.2 us
    all_to_all x1, blocking collectives, sum_over_row(): pieces = lax.all_to_all(pieces, NEAR, 0, 0, tiled=True)  23 us
    all_to_all x1, blocking collectives, sum_over_row(): return lax.all_to_all(copies, NEAR, 0, 0, tiled=True).reshape(rows, columns)  14.5 us
    pallas_call x1, Pallas kernels, local_part(): pl.pallas_call(local_kernel, in_specs=[HBM] * 4, out_specs=[VMEM] * 3, ou...  4.02 us
    ppermute x1, starting transfers between devices, on_device(): other = lax.ppermute(three_center, 'col', [(0, 1), (1, 0)])  1.91 us
  transfers between devices with their start and end apart: 1, of which 1 were waited for; matrix products, arithmetic and copies ran while one was open for 0% of the time, Pallas kernels for 6%

profile of v5, /device:TPU:8, one launch (start us, length us, event | category | flops | bytes accessed | tf_op | source)
XLA Modules:
  0.0 73.1 jit_solution(11166852724105821904)
XLA Ops:
  0.0 1.9 %collective-permute-start = (bf16[32,128,256]{2,1,0:T(8,128)(2,1)}, bf16[32,128,256]{2,1,0:T(8,128)(2,1)S(1)}, u32[]{:S(2)}, u32[]{:S(2)}) collective-permute-start(bf16[32,128,256]{2,1,0:T(8,128)(2,1)} %x_hbm.1), channel_id=1, source_target_pairs={{0,1},{1,0},{2,3},{3,2},{4,5},{5,4},{6,7},{7,6},{8,9},{9,8},{10,11... | collective-permute-start | bytes 6291464 | tf_op jit(solution)/shard_map/ppermute | solution.py:128
  1.9 4.0 %shard_map.46 = (bf16[4096,256]{1,0:T(8,128)(2,1)S(1)}, bf16[256,256]{1,0:T(8,128)(2,1)S(1)}, bf16[32,128,128]{2,1,0:T(8,128)(2,1)S(1)}) custom-call(s32[2,32]{1,0:T(2,128)} %bitcast.5, bf16[128,128]{1,0:T(8,128)(2,1)} %occ_hbm.1, bf16[128,128]{1,0:T(8,128)(2,1)} %virt_hbm.1, bf16[32,128,256]{2,1,0:T(8,128)(2,1)} %x_hbm.1), custom_call_target="tpu_custom_call" | custom-call | tf_op jit(solution)/shard_map/pallas_call | solution.py:69
  5.9 0.3 collective-permute-done.x_ref
  6.3 1.3 %shard_map.47 = bf16[256,512]{1,0:T(8,128)(2,1)S(1)} custom-call(bf16[32,128,128]{2,1,0:T(8,128)(2,1)S(1)} %get-tuple-element.8.kept_ref, bf16[32,128,256]{2,1,0:T(8,128)(2,1)S(1)} %collective-permute-done.x_ref, bf16[4096,256]{1,0:T(8,128)(2,1)S(1)} %get-tuple-element.9.occ_ref, bf16[256,256]{1,0:T(8,128)(2,1)S(1)} %get-tuple-element.10.here_ref), custom_call_target="tpu_custom_call" | custom-call | tf_op jit(solution)/shard_map/pallas_call | solution.py:104
  7.5 23.0 %all_to_all.15 = bf16[32,8,512]{2,1,0:T(8,128)(2,1)S(1)} all-to-all(bf16[32,8,512]{2,1,0:T(8,128)(2,1)S(1)} %bitcast.4), channel_id=1, replica_groups=mesh['z_hi'=3,'z_lo'=4,'y_hi'=4,'y_lo'=2,'x'=4,'col'=2] {'y_lo','x','z_lo'}, dimensions={0} | all-to-all | bytes 524288 | tf_op jit(solution)/shard_map/all_to_all | solution.py:117
  30.5 0.1 reduce_sum.24
  30.6 27.2 %all_to_all.16 = bf16[12,8,512]{2,1,0:T(8,128)(2,1)S(1)} all-to-all(bf16[12,8,512]{2,1,0:T(8,128)(2,1)S(1)} %broadcast_in_dim.4), channel_id=1, replica_groups=mesh['z_hi'=3,'z_lo'=4,'y_hi'=4,'y_lo'=2,'x'=4,'col'=2] {'y_hi','z_hi'}, dimensions={0} | all-to-all | bytes 196608 | tf_op jit(solution)/shard_map/all_to_all | solution.py:120
  57.8 14.5 %all_to_all.17 = bf16[32,8,512]{2,1,0:T(8,128)(2,1)S(1)} all-to-all(bf16[32,8,512]{2,1,0:T(8,128)(2,1)S(1)} %broadcast_in_dim.5), channel_id=1, replica_groups=mesh['z_hi'=3,'z_lo'=4,'y_hi'=4,'y_lo'=2,'x'=4,'col'=2] {'y_lo','x','z_lo'}, dimensions={0} | all-to-all | bytes 524288 | tf_op jit(solution)/shard_map/all_to_all | solution.py:123
  72.3 0.9 %multiply_bitcast_fusion = f32[256,512]{1,0:T(8,128)} fusion(bf16[32,8,512]{2,1,0:T(8,128)(2,1)S(1)} %all_to_all.17), kind=kLoop, calls=%fused_computation | loop fusion | flops 393216 | bytes 786432 | tf_op jit(solution)/shard_map/div | solution.py:132
  (3 shorter events, 0.1 us)
Async XLA Ops:
  0.0 6.3 %collective-permute-start = (bf16[32,128,256]{2,1,0:T(8,128)(2,1)}, bf16[32,128,256]{2,1,0:T(8,128)(2,1)S(1)}, u32[]{:S(2)}, u32[]{:S(2)}) collective-permute-start(bf16[32,128,256]{2,1,0:T(8,128)(2,1)} %x_hbm.1), channel_id=1, source_target_pairs={{0,1},{1,0},{2,3},{3,2},{4,5},{5,4},{6,7},{7,6},{8,9},{9,8},{10,11... | collective-permute-start | bytes 6291464 | tf_op jit(solution)/shard_map/ppermute | solution.py:128

commit v6 on v4

--- a/solution.py
+++ b/solution.py
@@ -85,28 +85,24 @@
     )(*[pltpu.with_memory_space_constraint(a, pltpu.HBM) for a in args])
 
 
-def remote_kernel(kept_ref, x_ref, occ_ref, here_ref, out_ref, virt):
-    count, width, own = x_ref.shape
+def remote_kernel(kept_ref, x_ref, occ_ref, out_ref, virt):
+    count, width, _ = x_ref.shape
     for m in range(count):
         side = jnp.dot(kept_ref[m], x_ref[m], preferred_element_type=jnp.float32)
         virt[m * width : (m + 1) * width, :] = side.astype(jnp.bfloat16)
-    there = transposed_dot(occ_ref[...], virt[...]).astype(jnp.bfloat16)
-    here = here_ref[...]
-    first = lax.axis_index("col") == 0
-    out_ref[:, :own] = jnp.where(first, here, there)
-    out_ref[:, own:] = jnp.where(first, there, here)
+    out_ref[...] = transposed_dot(occ_ref[...], virt[...]).astype(jnp.bfloat16)
 
 
-def remote_part(other, kept, occ_side, here):
+def remote_part(other, kept, occ_side):
     count, width, own = other.shape
     return pl.pallas_call(
         remote_kernel,
-        in_specs=[VMEM] * 4,
+        in_specs=[VMEM] * 3,
         out_specs=VMEM,
-        out_shape=jax.ShapeDtypeStruct((own, 2 * own), jnp.bfloat16),
+        out_shape=jax.ShapeDtypeStruct((own, own), jnp.bfloat16),
         scratch_shapes=[pltpu.VMEM((count * width, own), jnp.bfloat16)],
         compiler_params=PARAMS,
-    )(kept, other, occ_side, here)
+    )(kept, other, occ_side)
 
 
 def sum_over_row(partial):
@@ -125,8 +121,12 @@
     mu_dev, width, _ = three_center.shape
     other = lax.ppermute(three_center, "col", [(0, 1), (1, 0)])
     occ_side, here, kept = local_part(three_center, screen_mask.T, green_occ, green_virt)
-    partial = remote_part(other, kept, occ_side, here)
-    summed = sum_over_row(partial).astype(jnp.float32)
+    there = remote_part(other, kept, occ_side)
+    here, there = sum_over_row(here), sum_over_row(there)
+    first = lax.axis_index("col") == 0
+    summed = jnp.concatenate(
+        [jnp.where(first, here, there), jnp.where(first, there, here)], axis=1
+    ).astype(jnp.float32)
     return -summed / jnp.sqrt(jnp.float32(mu_dev * Z * YX * width))
 
 

time: 73 us -> 116 us (1.59)
  blocking collectives: 64.3 us -> 0 us
  waiting for transfers between devices: 0.31 us -> 57.4 us
  starting transfers between devices: 1.91 us -> 44.5 us
  local copies, waits for them, and re-layouts: 0.03 us -> 5.49 us
  Pallas kernels: 5.28 us -> 6.58 us
    all_to_all x3 -> x0, blocking collectives: 64.3 us -> none  [the longest x1 25 us: sum_over_row(): pieces = lax.all_to_all(pieces, 'yx', 0, 0, tiled=True)]
    all_to_all x0 -> x6, waiting for transfers between devices: none -> 57.4 us  [the longest x2 21.5 us: sum_over_row(): copies = lax.all_to_all(copies, 'z', 0, 0, tiled=True)]
    all_to_all x0 -> x6, starting transfers between devices: none -> 42.6 us  [the longest x2 17.7 us: sum_over_row(): pieces = lax.all_to_all(pieces, 'yx', 0, 0, tiled=True)]
    unnamed x0 -> x4, local copies, waits for them, and re-layouts: none -> 2.92 us
    broadcast_in_dim x1 -> x2, local copies, waits for them, and re-layouts: 0.02 us -> 1.33 us  [sum_over_row(): copies = jnp.broadcast_to(total[None], (YX,) + total.shape)]
    broadcast_in_dim x1 -> x2, local copies, waits for them, and re-layouts: 0.01 us -> 1.25 us  [sum_over_row(): copies = jnp.broadcast_to(piece[None], (Z,) + piece.shape)]
  transfers between devices with their start and end apart: 1 -> 7, of which waited for: 1 -> 6; matrix products, arithmetic and copies ran while one was open for 0% -> 0% of each run, Pallas kernels for 6% -> 6%
where the time goes in v6:
time: 116 us; the launch traced here: 115 us
  waiting for transfers between devices  57.4 us (49%)
  starting transfers between devices  44.5 us (38%)
  Pallas kernels  6.58 us (6%)
  local copies, waits for them, and re-layouts  5.49 us (5%)
    all_to_all x2, waiting for transfers between devices, sum_over_row(): copies = lax.all_to_all(copies, 'z', 0, 0, tiled=True)  21.5 us
    all_to_all x2, waiting for transfers between devices, sum_over_row(): return lax.all_to_all(copies, 'yx', 0, 0, tiled=True).reshape(rows, columns)  19.2 us
    all_to_all x2, starting transfers between devices, sum_over_row(): pieces = lax.all_to_all(pieces, 'yx', 0, 0, tiled=True)  17.7 us
    all_to_all x2, waiting for transfers between devices, sum_over_row(): pieces = lax.all_to_all(pieces, 'yx', 0, 0, tiled=True)  16.7 us
    all_to_all x2, starting transfers between devices, sum_over_row(): copies = lax.all_to_all(copies, 'z', 0, 0, tiled=True)  15.4 us
    all_to_all x2, starting transfers between devices, sum_over_row(): return lax.all_to_all(copies, 'yx', 0, 0, tiled=True).reshape(rows, columns)  9.57 us
    pallas_call x1, Pallas kernels, local_part(): pl.pallas_call(local_kernel, in_specs=[HBM] * 4, out_specs=[VMEM] * 3, ou...  4.68 us
    unnamed x4, local copies, waits for them, and re-layouts  2.92 us
  transfers between devices with their start and end apart: 7, of which 6 were waited for; matrix products, arithmetic and copies ran while one was open for 0% of the time, Pallas kernels for 6%

profile of v6, /device:TPU:8, one launch (start us, length us, event | category | flops | bytes accessed | tf_op | source)
XLA Modules:
  0.0 115.1 jit_solution(4126026650409033125)
XLA Ops:
  0.0 1.9 %collective-permute-start = (bf16[32,128,256]{2,1,0:T(8,128)(2,1)}, bf16[32,128,256]{2,1,0:T(8,128)(2,1)S(1)}, u32[]{:S(2)}, u32[]{:S(2)}) collective-permute-start(bf16[32,128,256]{2,1,0:T(8,128)(2,1)} %x_hbm.1), channel_id=1, source_target_pairs={{0,1},{1,0},{2,3},{3,2},{4,5},{5,4},{6,7},{7,6},{8,9},{9,8},{10,11... | collective-permute-start | bytes 6291464 | tf_op jit(solution)/shard_map/ppermute | solution.py:122
  1.9 4.7 %shard_map.46 = (bf16[4096,256]{1,0:T(8,128)(2,1)S(1)}, bf16[256,256]{1,0:T(8,128)(2,1)}, bf16[32,128,128]{2,1,0:T(8,128)(2,1)S(1)}) custom-call(s32[2,32]{1,0:T(2,128)} %bitcast.7, bf16[128,128]{1,0:T(8,128)(2,1)} %occ_hbm.1, bf16[128,128]{1,0:T(8,128)(2,1)} %virt_hbm.1, bf16[32,128,256]{2,1,0:T(8,128)(2,1)} %x_hbm.1), custom_call_target="tpu_custom_call" | custom-call | tf_op jit(solution)/shard_map/pallas_call | solution.py:67
  6.6 0.0 copy-start
  6.6 1.3 %copy-done = bf16[4096,256]{1,0:T(8,128)(2,1)} copy-done((bf16[4096,256]{1,0:T(8,128)(2,1)}, bf16[4096,256]{1,0:T(8,128)(2,1)S(1)}, u32[]{:S(2)}) %copy-start) | copy-done | bytes 2097176
  7.9 13.0 %all-to-all-start = ((bf16[32,8,256]{2,1,0:T(8,128)(2,1)}), bf16[32,8,256]{2,1,0:T(8,128)(2,1)S(1)}, u32[]{:S(2)}, u32[]{:S(2)}) async-start(bf16[32,8,256]{2,1,0:T(8,128)(2,1)} %bitcast.1), calls=%async_computation | async-start | bytes 262144 | tf_op jit(solution)/shard_map/all_to_all | solution.py:111
  20.9 0.0 collective-permute-done.x_ref
  20.9 0.0 copy-start.1
  21.0 1.6 %copy-done.1 = bf16[4096,256]{1,0:T(8,128)(2,1)S(1)} copy-done((bf16[4096,256]{1,0:T(8,128)(2,1)S(1)}, bf16[4096,256]{1,0:T(8,128)(2,1)}, u32[]{:S(2)}) %copy-start.1) | copy-done | bytes 2097176
  22.5 1.9 %shard_map.47 = bf16[256,256]{1,0:T(8,128)(2,1)} custom-call(bf16[32,128,128]{2,1,0:T(8,128)(2,1)S(1)} %get-tuple-element.9.kept_ref, bf16[32,128,256]{2,1,0:T(8,128)(2,1)S(1)} %collective-permute-done.x_ref, bf16[4096,256]{1,0:T(8,128)(2,1)S(1)} %copy-done.1), custom_call_target="tpu_custom_call" | custom-call | tf_op jit(solution)/shard_map/pallas_call | solution.py:98
  24.4 7.1 %all-to-all-done = bf16[32,8,256]{2,1,0:T(8,128)(2,1)S(1)} async-done(((bf16[32,8,256]{2,1,0:T(8,128)(2,1)}), bf16[32,8,256]{2,1,0:T(8,128)(2,1)S(1)}, u32[]{:S(2)}, u32[]{:S(2)}) %all-to-all-start) | async-done | bytes 131104 | tf_op jit(solution)/shard_map/all_to_all | solution.py:111
  31.6 4.7 %all-to-all-start.3 = ((bf16[32,8,256]{2,1,0:T(8,128)(2,1)}), bf16[32,8,256]{2,1,0:T(8,128)(2,1)S(1)}, u32[]{:S(2)}, u32[]{:S(2)}) async-start(bf16[32,8,256]{2,1,0:T(8,128)(2,1)} %bitcast.2), calls=%async_computation.3 | async-start | bytes 262144 | tf_op jit(solution)/shard_map/all_to_all | solution.py:111
  36.3 9.6 %all-to-all-done.3 = bf16[32,8,256]{2,1,0:T(8,128)(2,1)S(1)} async-done(((bf16[32,8,256]{2,1,0:T(8,128)(2,1)}), bf16[32,8,256]{2,1,0:T(8,128)(2,1)S(1)}, u32[]{:S(2)}, u32[]{:S(2)}) %all-to-all-start.3) | async-done | bytes 131104 | tf_op jit(solution)/shard_map/all_to_all | solution.py:111
  45.9 0.6 broadcast_in_dim.8
  46.5 11.9 %all-to-all-start.1 = ((bf16[12,8,256]{2,1,0:T(8,128)(2,1)}), bf16[12,8,256]{2,1,0:T(8,128)(2,1)S(1)}, u32[]{:S(2)}, u32[]{:S(2)}) async-start(bf16[12,8,256]{2,1,0:T(8,128)(2,1)} %broadcast_in_dim.8), calls=%async_computation.1 | async-start | bytes 98304 | tf_op jit(solution)/shard_map/all_to_all | solution.py:114
  58.4 10.8 %all-to-all-done.1 = bf16[12,8,256]{2,1,0:T(8,128)(2,1)S(1)} async-done(((bf16[12,8,256]{2,1,0:T(8,128)(2,1)}), bf16[12,8,256]{2,1,0:T(8,128)(2,1)S(1)}, u32[]{:S(2)}, u32[]{:S(2)}) %all-to-all-start.1) | async-done | bytes 49184 | tf_op jit(solution)/shard_map/all_to_all | solution.py:114
  69.2 0.6 broadcast_in_dim.10
  69.8 3.5 %all-to-all-start.4 = ((bf16[12,8,256]{2,1,0:T(8,128)(2,1)}), bf16[12,8,256]{2,1,0:T(8,128)(2,1)S(1)}, u32[]{:S(2)}, u32[]{:S(2)}) async-start(bf16[12,8,256]{2,1,0:T(8,128)(2,1)} %broadcast_in_dim.10), calls=%async_computation.4 | async-start | bytes 98304 | tf_op jit(solution)/shard_map/all_to_all | solution.py:114
  73.4 10.7 %all-to-all-done.4 = bf16[12,8,256]{2,1,0:T(8,128)(2,1)S(1)} async-done(((bf16[12,8,256]{2,1,0:T(8,128)(2,1)}), bf16[12,8,256]{2,1,0:T(8,128)(2,1)S(1)}, u32[]{:S(2)}, u32[]{:S(2)}) %all-to-all-start.4) | async-done | bytes 49184 | tf_op jit(solution)/shard_map/all_to_all | solution.py:114
  84.1 0.7 broadcast_in_dim.9
  84.7 4.8 %all-to-all-start.2 = ((bf16[32,8,256]{2,1,0:T(8,128)(2,1)}), bf16[32,8,256]{2,1,0:T(8,128)(2,1)S(1)}, u32[]{:S(2)}, u32[]{:S(2)}) async-start(bf16[32,8,256]{2,1,0:T(8,128)(2,1)} %broadcast_in_dim.9), calls=%async_computation.2 | async-start | bytes 262144 | tf_op jit(solution)/shard_map/all_to_all | solution.py:117
  89.6 9.6 %all-to-all-done.2 = bf16[32,8,256]{2,1,0:T(8,128)(2,1)S(1)} async-done(((bf16[32,8,256]{2,1,0:T(8,128)(2,1)}), bf16[32,8,256]{2,1,0:T(8,128)(2,1)S(1)}, u32[]{:S(2)}, u32[]{:S(2)}) %all-to-all-start.2) | async-done | bytes 131104 | tf_op jit(solution)/shard_map/all_to_all | solution.py:117
  99.1 0.7 broadcast_in_dim.11
  99.8 4.8 %all-to-all-start.5 = ((bf16[32,8,256]{2,1,0:T(8,128)(2,1)}), bf16[32,8,256]{2,1,0:T(8,128)(2,1)S(1)}, u32[]{:S(2)}, u32[]{:S(2)}) async-start(bf16[32,8,256]{2,1,0:T(8,128)(2,1)} %broadcast_in_dim.11), calls=%async_computation.5 | async-start | bytes 262144 | tf_op jit(solution)/shard_map/all_to_all | solution.py:117
  104.6 9.6 %all-to-all-done.5 = bf16[32,8,256]{2,1,0:T(8,128)(2,1)S(1)} async-done(((bf16[32,8,256]{2,1,0:T(8,128)(2,1)}), bf16[32,8,256]{2,1,0:T(8,128)(2,1)S(1)}, u32[]{:S(2)}, u32[]{:S(2)}) %all-to-all-start.5) | async-done | bytes 131104 | tf_op jit(solution)/shard_map/all_to_all | solution.py:117
  114.3 0.9 negate_multiply_fusion
  (5 shorter events, 0.1 us)
Async XLA Ops:
  0.0 20.9 %collective-permute-start = (bf16[32,128,256]{2,1,0:T(8,128)(2,1)}, bf16[32,128,256]{2,1,0:T(8,128)(2,1)S(1)}, u32[]{:S(2)}, u32[]{:S(2)}) collective-permute-start(bf16[32,128,256]{2,1,0:T(8,128)(2,1)} %x_hbm.1), channel_id=1, source_target_pairs={{0,1},{1,0},{2,3},{3,2},{4,5},{5,4},{6,7},{7,6},{8,9},{9,8},{10,11... | collective-permute-start | bytes 6291464 | tf_op jit(solution)/shard_map/ppermute | solution.py:122
  6.6 1.3 %copy-start = (bf16[4096,256]{1,0:T(8,128)(2,1)}, bf16[4096,256]{1,0:T(8,128)(2,1)S(1)}, u32[]{:S(2)}) copy-start(bf16[4096,256]{1,0:T(8,128)(2,1)S(1)} %get-tuple-element.10.occ_ref) | copy-start | bytes 6291460
  7.9 23.6 %all-to-all-start = ((bf16[32,8,256]{2,1,0:T(8,128)(2,1)}), bf16[32,8,256]{2,1,0:T(8,128)(2,1)S(1)}, u32[]{:S(2)}, u32[]{:S(2)}) async-start(bf16[32,8,256]{2,1,0:T(8,128)(2,1)} %bitcast.1), calls=%async_computation | async-start | bytes 262144 | tf_op jit(solution)/shard_map/all_to_all | solution.py:111
  20.9 1.6 %copy-start.1 = (bf16[4096,256]{1,0:T(8,128)(2,1)S(1)}, bf16[4096,256]{1,0:T(8,128)(2,1)}, u32[]{:S(2)}) copy-start(bf16[4096,256]{1,0:T(8,128)(2,1)} %copy-done) | copy-start | bytes 6291460
  31.6 14.3 %all-to-all-start.3 = ((bf16[32,8,256]{2,1,0:T(8,128)(2,1)}), bf16[32,8,256]{2,1,0:T(8,128)(2,1)S(1)}, u32[]{:S(2)}, u32[]{:S(2)}) async-start(bf16[32,8,256]{2,1,0:T(8,128)(2,1)} %bitcast.2), calls=%async_computation.3 | async-start | bytes 262144 | tf_op jit(solution)/shard_map/all_to_all | solution.py:111
  46.5 22.7 %all-to-all-start.1 = ((bf16[12,8,256]{2,1,0:T(8,128)(2,1)}), bf16[12,8,256]{2,1,0:T(8,128)(2,1)S(1)}, u32[]{:S(2)}, u32[]{:S(2)}) async-start(bf16[12,8,256]{2,1,0:T(8,128)(2,1)} %broadcast_in_dim.8), calls=%async_computation.1 | async-start | bytes 98304 | tf_op jit(solution)/shard_map/all_to_all | solution.py:114
  69.8 14.2 %all-to-all-start.4 = ((bf16[12,8,256]{2,1,0:T(8,128)(2,1)}), bf16[12,8,256]{2,1,0:T(8,128)(2,1)S(1)}, u32[]{:S(2)}, u32[]{:S(2)}) async-start(bf16[12,8,256]{2,1,0:T(8,128)(2,1)} %broadcast_in_dim.10), calls=%async_computation.4 | async-start | bytes 98304 | tf_op jit(solution)/shard_map/all_to_all | solution.py:114
  84.7 14.4 %all-to-all-start.2 = ((bf16[32,8,256]{2,1,0:T(8,128)(2,1)}), bf16[32,8,256]{2,1,0:T(8,128)(2,1)S(1)}, u32[]{:S(2)}, u32[]{:S(2)}) async-start(bf16[32,8,256]{2,1,0:T(8,128)(2,1)} %broadcast_in_dim.9), calls=%async_computation.2 | async-start | bytes 262144 | tf_op jit(solution)/shard_map/all_to_all | solution.py:117
  99.8 14.4 %all-to-all-start.5 = ((bf16[32,8,256]{2,1,0:T(8,128)(2,1)}), bf16[32,8,256]{2,1,0:T(8,128)(2,1)S(1)}, u32[]{:S(2)}, u32[]{:S(2)}) async-start(bf16[32,8,256]{2,1,0:T(8,128)(2,1)} %broadcast_in_dim.11), calls=%async_computation.5 | async-start | bytes 262144 | tf_op jit(solution)/shard_map/all_to_all | solution.py:117

commit v7 on v4

--- a/solution.py
+++ b/solution.py
@@ -115,7 +115,7 @@
     pieces = lax.all_to_all(pieces, "yx", 0, 0, tiled=True)
     piece = jnp.sum(pieces.astype(jnp.float32), axis=0).astype(jnp.bfloat16)
     copies = jnp.broadcast_to(piece[None], (Z,) + piece.shape)
-    copies = lax.all_to_all(copies, "z", 0, 0, tiled=True)
+    copies = lax.all_to_all(copies, ("z_lo", "z_hi"), 0, 0, tiled=True)
     total = jnp.sum(copies.astype(jnp.float32), axis=0).astype(jnp.bfloat16)
     copies = jnp.broadcast_to(total[None], (YX,) + total.shape)
     return lax.all_to_all(copies, "yx", 0, 0, tiled=True).reshape(rows, columns)
@@ -131,11 +131,12 @@
 
 
 def solution(mesh):
-    fine = Mesh(mesh.devices.reshape(Z, YX, 2), ("z", "yx", "col"))
+    row = ("z_hi", "z_lo", "yx")
+    fine = Mesh(mesh.devices.reshape(Z // 2, 2, YX, 2), ("z_hi", "z_lo", "yx", "col"))
     return jax.shard_map(
         on_device,
         mesh=fine,
-        in_specs=(P(("z", "yx"), None, "col"), P(("z", "yx"), None), P(), P()),
+        in_specs=(P(row, None, "col"), P(row, None), P(), P()),
         out_specs=P("col", None),
         check_vma=False,
     )

time: 73 us -> 72 us (0.986)
  blocking collectives: 64.3 us -> 63.2 us
    all_to_all x1, blocking collectives: 24.1 us -> 23 us  [sum_over_row(): copies = lax.all_to_all(copies, ('z_lo', 'z_hi'), 0, 0, tiled=True)]
where the time goes in v7:
time: 72 us; the launch traced here: 71.7 us
  blocking collectives  63.2 us (88%)
  Pallas kernels  5.28 us (7%)
  starting transfers between devices  1.91 us (3%)
  other arithmetic  0.93 us (1%)
    all_to_all x1, blocking collectives, sum_over_row(): pieces = lax.all_to_all(pieces, 'yx', 0, 0, tiled=True)  25 us
    all_to_all x1, blocking collectives, sum_over_row(): copies = lax.all_to_all(copies, ('z_lo', 'z_hi'), 0, 0, tiled=True)  23 us
    all_to_all x1, blocking collectives, sum_over_row(): return lax.all_to_all(copies, 'yx', 0, 0, tiled=True).reshape(rows, columns)  15.2 us
    pallas_call x1, Pallas kernels, local_part(): pl.pallas_call(local_kernel, in_specs=[HBM] * 4, out_specs=[VMEM] * 3, ou...  4.02 us
    ppermute x1, starting transfers between devices, on_device(): other = lax.ppermute(three_center, 'col', [(0, 1), (1, 0)])  1.91 us
  transfers between devices with their start and end apart: 1, of which 1 were waited for; matrix products, arithmetic and copies ran while one was open for 0% of the time, Pallas kernels for 6%

profile of v7, /device:TPU:8, one launch (start us, length us, event | category | flops | bytes accessed | tf_op | source)
XLA Modules:
  0.0 71.7 jit_solution(14256843587862614452)
XLA Ops:
  0.0 1.9 %collective-permute-start = (bf16[32,128,256]{2,1,0:T(8,128)(2,1)}, bf16[32,128,256]{2,1,0:T(8,128)(2,1)S(1)}, u32[]{:S(2)}, u32[]{:S(2)}) collective-permute-start(bf16[32,128,256]{2,1,0:T(8,128)(2,1)} %x_hbm.1), channel_id=1, source_target_pairs={{0,1},{1,0},{2,3},{3,2},{4,5},{5,4},{6,7},{7,6},{8,9},{9,8},{10,11... | collective-permute-start | bytes 6291464 | tf_op jit(solution)/shard_map/ppermute | solution.py:126
  1.9 4.0 %shard_map.46 = (bf16[4096,256]{1,0:T(8,128)(2,1)S(1)}, bf16[256,256]{1,0:T(8,128)(2,1)S(1)}, bf16[32,128,128]{2,1,0:T(8,128)(2,1)S(1)}) custom-call(s32[2,32]{1,0:T(2,128)} %bitcast.5, bf16[128,128]{1,0:T(8,128)(2,1)} %occ_hbm.1, bf16[128,128]{1,0:T(8,128)(2,1)} %virt_hbm.1, bf16[32,128,256]{2,1,0:T(8,128)(2,1)} %x_hbm.1), custom_call_target="tpu_custom_call" | custom-call | tf_op jit(solution)/shard_map/pallas_call | solution.py:67
  5.9 0.3 collective-permute-done.x_ref
  6.3 1.3 %shard_map.47 = bf16[256,512]{1,0:T(8,128)(2,1)S(1)} custom-call(bf16[32,128,128]{2,1,0:T(8,128)(2,1)S(1)} %get-tuple-element.8.kept_ref, bf16[32,128,256]{2,1,0:T(8,128)(2,1)S(1)} %collective-permute-done.x_ref, bf16[4096,256]{1,0:T(8,128)(2,1)S(1)} %get-tuple-element.9.occ_ref, bf16[256,256]{1,0:T(8,128)(2,1)S(1)} %get-tuple-element.10.here_ref), custom_call_target="tpu_custom_call" | custom-call | tf_op jit(solution)/shard_map/pallas_call | solution.py:102
  7.5 25.0 %all_to_all.15 = bf16[32,8,512]{2,1,0:T(8,128)(2,1)S(1)} all-to-all(bf16[32,8,512]{2,1,0:T(8,128)(2,1)S(1)} %bitcast.4), channel_id=1, replica_groups=mesh['z_hi'=6,'z_lo'=2,'yx'=32,'col'=2] {'yx'}, dimensions={0} | all-to-all | bytes 524288 | tf_op jit(solution)/shard_map/all_to_all | solution.py:115
  32.5 0.1 reduce_sum.24
  32.6 23.0 %all_to_all.16 = bf16[12,8,512]{2,1,0:T(8,128)(2,1)S(1)} all-to-all(bf16[12,8,512]{2,1,0:T(8,128)(2,1)S(1)} %broadcast_in_dim.4), channel_id=1, replica_groups=mesh['z_hi'=6,'z_lo'=2,'yx'=32,'col'=2] {'z_lo','z_hi'}, dimensions={0} | all-to-all | bytes 196608 | tf_op jit(solution)/shard_map/all_to_all | solution.py:118
  55.6 15.2 %all_to_all.17 = bf16[32,8,512]{2,1,0:T(8,128)(2,1)S(1)} all-to-all(bf16[32,8,512]{2,1,0:T(8,128)(2,1)S(1)} %broadcast_in_dim.5), channel_id=1, replica_groups=mesh['z_hi'=6,'z_lo'=2,'yx'=32,'col'=2] {'yx'}, dimensions={0} | all-to-all | bytes 524288 | tf_op jit(solution)/shard_map/all_to_all | solution.py:121
  70.9 0.9 %multiply_bitcast_fusion = f32[256,512]{1,0:T(8,128)} fusion(bf16[32,8,512]{2,1,0:T(8,128)(2,1)S(1)} %all_to_all.17), kind=kLoop, calls=%fused_computation | loop fusion | flops 393216 | bytes 786432 | tf_op jit(solution)/shard_map/div | solution.py:130
  (3 shorter events, 0.1 us)
Async XLA Ops:
  0.0 6.3 %collective-permute-start = (bf16[32,128,256]{2,1,0:T(8,128)(2,1)}, bf16[32,128,256]{2,1,0:T(8,128)(2,1)S(1)}, u32[]{:S(2)}, u32[]{:S(2)}) collective-permute-start(bf16[32,128,256]{2,1,0:T(8,128)(2,1)} %x_hbm.1), channel_id=1, source_target_pairs={{0,1},{1,0},{2,3},{3,2},{4,5},{5,4},{6,7},{7,6},{8,9},{9,8},{10,11... | collective-permute-start | bytes 6291464 | tf_op jit(solution)/shard_map/ppermute | solution.py:126

commit v8 on v7

--- a/solution.py
+++ b/solution.py
@@ -132,7 +132,7 @@
 
 def solution(mesh):
     row = ("z_hi", "z_lo", "yx")
-    fine = Mesh(mesh.devices.reshape(Z // 2, 2, YX, 2), ("z_hi", "z_lo", "yx", "col"))
+    fine = Mesh(mesh.devices.reshape(Z // 3, 3, YX, 2), ("z_hi", "z_lo", "yx", "col"))
     return jax.shard_map(
         on_device,
         mesh=fine,

time: 72 us -> 72.4 us (level)
  no operation moved by 1% of the time
where the time goes in v8:
time: 72.4 us; the launch traced here: 72.1 us
  blocking collectives  63.6 us (88%)
  Pallas kernels  5.28 us (7%)
  starting transfers between devices  1.91 us (3%)
  other arithmetic  0.93 us (1%)
    all_to_all x1, blocking collectives, sum_over_row(): pieces = lax.all_to_all(pieces, 'yx', 0, 0, tiled=True)  25 us
    all_to_all x1, blocking collectives, sum_over_row(): copies = lax.all_to_all(copies, ('z_lo', 'z_hi'), 0, 0, tiled=True)  23.4 us
    all_to_all x1, blocking collectives, sum_over_row(): return lax.all_to_all(copies, 'yx', 0, 0, tiled=True).reshape(rows, columns)  15.2 us
    pallas_call x1, Pallas kernels, local_part(): pl.pallas_call(local_kernel, in_specs=[HBM] * 4, out_specs=[VMEM] * 3, ou...  4.02 us
    ppermute x1, starting transfers between devices, on_device(): other = lax.ppermute(three_center, 'col', [(0, 1), (1, 0)])  1.91 us
  transfers between devices with their start and end apart: 1, of which 1 were waited for; matrix products, arithmetic and copies ran while one was open for 0% of the time, Pallas kernels for 6%

profile of v8, /device:TPU:8, one launch (start us, length us, event | category | flops | bytes accessed | tf_op | source)
XLA Modules:
  0.0 72.1 jit_solution(2559753452066322958)
XLA Ops:
  0.0 1.9 %collective-permute-start = (bf16[32,128,256]{2,1,0:T(8,128)(2,1)}, bf16[32,128,256]{2,1,0:T(8,128)(2,1)S(1)}, u32[]{:S(2)}, u32[]{:S(2)}) collective-permute-start(bf16[32,128,256]{2,1,0:T(8,128)(2,1)} %x_hbm.1), channel_id=1, source_target_pairs={{0,1},{1,0},{2,3},{3,2},{4,5},{5,4},{6,7},{7,6},{8,9},{9,8},{10,11... | collective-permute-start | bytes 6291464 | tf_op jit(solution)/shard_map/ppermute | solution.py:126
  1.9 4.0 %shard_map.46 = (bf16[4096,256]{1,0:T(8,128)(2,1)S(1)}, bf16[256,256]{1,0:T(8,128)(2,1)S(1)}, bf16[32,128,128]{2,1,0:T(8,128)(2,1)S(1)}) custom-call(s32[2,32]{1,0:T(2,128)} %bitcast.5, bf16[128,128]{1,0:T(8,128)(2,1)} %occ_hbm.1, bf16[128,128]{1,0:T(8,128)(2,1)} %virt_hbm.1, bf16[32,128,256]{2,1,0:T(8,128)(2,1)} %x_hbm.1), custom_call_target="tpu_custom_call" | custom-call | tf_op jit(solution)/shard_map/pallas_call | solution.py:67
  5.9 0.3 collective-permute-done.x_ref
  6.3 1.3 %shard_map.47 = bf16[256,512]{1,0:T(8,128)(2,1)S(1)} custom-call(bf16[32,128,128]{2,1,0:T(8,128)(2,1)S(1)} %get-tuple-element.8.kept_ref, bf16[32,128,256]{2,1,0:T(8,128)(2,1)S(1)} %collective-permute-done.x_ref, bf16[4096,256]{1,0:T(8,128)(2,1)S(1)} %get-tuple-element.9.occ_ref, bf16[256,256]{1,0:T(8,128)(2,1)S(1)} %get-tuple-element.10.here_ref), custom_call_target="tpu_custom_call" | custom-call | tf_op jit(solution)/shard_map/pallas_call | solution.py:102
  7.5 25.0 %all_to_all.15 = bf16[32,8,512]{2,1,0:T(8,128)(2,1)S(1)} all-to-all(bf16[32,8,512]{2,1,0:T(8,128)(2,1)S(1)} %bitcast.4), channel_id=1, replica_groups=mesh['z_hi'=4,'z_lo'=3,'yx'=32,'col'=2] {'yx'}, dimensions={0} | all-to-all | bytes 524288 | tf_op jit(solution)/shard_map/all_to_all | solution.py:115
  32.5 0.1 reduce_sum.24
  32.6 23.4 %all_to_all.16 = bf16[12,8,512]{2,1,0:T(8,128)(2,1)S(1)} all-to-all(bf16[12,8,512]{2,1,0:T(8,128)(2,1)S(1)} %broadcast_in_dim.4), channel_id=1, replica_groups=mesh['z_hi'=4,'z_lo'=3,'yx'=32,'col'=2] {'z_lo','z_hi'}, dimensions={0} | all-to-all | bytes 196608 | tf_op jit(solution)/shard_map/all_to_all | solution.py:118
  56.1 15.2 %all_to_all.17 = bf16[32,8,512]{2,1,0:T(8,128)(2,1)S(1)} all-to-all(bf16[32,8,512]{2,1,0:T(8,128)(2,1)S(1)} %broadcast_in_dim.5), channel_id=1, replica_groups=mesh['z_hi'=4,'z_lo'=3,'yx'=32,'col'=2] {'yx'}, dimensions={0} | all-to-all | bytes 524288 | tf_op jit(solution)/shard_map/all_to_all | solution.py:121
  71.3 0.9 %multiply_bitcast_fusion = f32[256,512]{1,0:T(8,128)} fusion(bf16[32,8,512]{2,1,0:T(8,128)(2,1)S(1)} %all_to_all.17), kind=kLoop, calls=%fused_computation | loop fusion | flops 393216 | bytes 786432 | tf_op jit(solution)/shard_map/div | solution.py:130
  (3 shorter events, 0.1 us)
Async XLA Ops:
  0.0 6.3 %collective-permute-start = (bf16[32,128,256]{2,1,0:T(8,128)(2,1)}, bf16[32,128,256]{2,1,0:T(8,128)(2,1)S(1)}, u32[]{:S(2)}, u32[]{:S(2)}) collective-permute-start(bf16[32,128,256]{2,1,0:T(8,128)(2,1)} %x_hbm.1), channel_id=1, source_target_pairs={{0,1},{1,0},{2,3},{3,2},{4,5},{5,4},{6,7},{7,6},{8,9},{9,8},{10,11... | collective-permute-start | bytes 6291464 | tf_op jit(solution)/shard_map/ppermute | solution.py:126
